TPU v7x, 128 devices: a whole 4x4x4 slice. The times are simulated.
128 devices in a mesh: struct: 4 (over x), fluid: 32 (over z, y, core).
Axes of the slice: x: 4, y: 4, z: 4, core: 2. Of those that a mesh axis runs over, the one named last changes fastest.
Arguments:
- shell_motion: float32 [3, 1048576], P(None, ('struct', 'fluid')), may hold values from -6 to 6
- owner: int32 [1048576, 1], P(('struct', 'fluid')), may hold values from 0 to 127; in each aligned block of 8192 rows (0 to 8191, 8192 to 16383, ...) at most 128 rows name the same one
- stencil_slot: int32 [4, 8, 256, 128], P(None, 'struct', 'fluid'), may hold values from 0 to 16383
- stencil_weight: float32 [4, 8, 256, 128], P(None, 'struct', 'fluid'), may hold values from 0 to 0.5
- prev_motion: float32 [3, 8, 256, 256], P(None, 'struct', 'fluid'), may hold values from -6 to 6
- node_offset: float32 [3, 8, 256, 256], P(None, 'struct', 'fluid'), may hold values from -0.07 to 0.07
- cell_split: int32 [8, 256, 256], P('struct', 'fluid'), may hold values from 0 to 3
Outputs:
- mesh_motion: float32 [3, 8, 256, 256], P(None, 'struct', 'fluid')
Inputs may be any that keep to these rules, and one draw needn't show every extreme that they name: Among the 8192 shell nodes of one device, no owner is named by more than 128 of them, a bound that some block reaches.
All inputs are finite; a program needn't handle non-finite values.
Results may differ from a plain program's by a relative error of at most 0.0003.
Values sent between devices are 32-bit elements; how exact they have to be, the bound alone decides.
No kernel may reach another device: no remote copies, remote signals or barrier semaphores. Data moves between devices by JAX's collectives and lax.ppermute only.
A program may use at most 64 MiB of HBM per device.

v0:
```python
from functools import reduce
import jax
import jax.numpy as jnp
from jax import lax
from jax.sharding import PartitionSpec as P

SWEEPS = 4
LAMBDA_RATIO = 1.0
RELAX_FACTOR = 0.5
STEP_ORDERS = ((0, 1, 2), (0, 2, 1), (1, 0, 2), (1, 2, 0), (2, 0, 1), (2, 1, 0))
CORNER_LIST = tuple(
    ((shift_x, shift_y, shift_z) for shift_x in (0, 1) for shift_y in (0, 1) for shift_z in (0, 1))
)


def from_behind(block, axis, distance):
    devices = range(lax.axis_size(axis))
    route = [((i - distance) % len(devices), i) for i in devices]
    return lax.ppermute(block, axis, route)


def cross_product(left_vec, right_vec):
    return jnp.stack(
        [
            left_vec[1] * right_vec[2] - left_vec[2] * right_vec[1],
            left_vec[2] * right_vec[0] - left_vec[0] * right_vec[2],
            left_vec[0] * right_vec[1] - left_vec[1] * right_vec[0],
        ]
    )


def select_flip(flip_y, flip_z, unflipped, flipped_z, flipped_y, flipped_both):
    return jnp.where(
        flip_y, jnp.where(flip_z, flipped_both, flipped_y), jnp.where(flip_z, flipped_z, unflipped)
    )


def reflect_corners(corners, flip_y, flip_z):
    result = {}
    for corner in CORNER_LIST:
        shift_x, shift_y, shift_z = corner
        result[corner] = select_flip(
            flip_y,
            flip_z,
            corners[corner],
            corners[shift_x, shift_y, 1 - shift_z],
            corners[shift_x, 1 - shift_y, shift_z],
            corners[shift_x, 1 - shift_y, 1 - shift_z],
        )
    return result


def flip_masks(split_codes):
    flip_y = split_codes // 2 == 1
    flip_z = split_codes % 2 == 1
    sign_y = jnp.where(flip_y, -1.0, 1.0).astype(jnp.float32)
    sign_z = jnp.where(flip_z, -1.0, 1.0).astype(jnp.float32)
    return (flip_y, flip_z, sign_y, sign_z)


def lattice_edge(vertex, sign_y, sign_z):
    return jnp.stack(
        [jnp.full_like(sign_y, float(vertex[0])), sign_y * vertex[1], sign_z * vertex[2]]
    )


def element_gradients(offsets, step_order, sign_y, sign_z):
    position = [0, 0, 0]
    vertex_path = [(0, 0, 0)]
    for axis_id in step_order:
        position[axis_id] = 1
        vertex_path.append(tuple(position))
    anchor = offsets[vertex_path[0]]
    edge_list = [
        lattice_edge(vertex, sign_y, sign_z) + offsets[vertex] - anchor
        for vertex in vertex_path[1:]
    ]
    across_one = cross_product(edge_list[1], edge_list[2])
    across_two = cross_product(edge_list[2], edge_list[0])
    across_three = cross_product(edge_list[0], edge_list[1])
    volume_six = jnp.sum(edge_list[0] * across_one, axis=0)
    grad_one = across_one / volume_six
    grad_two = across_two / volume_six
    grad_three = across_three / volume_six
    grad_zero = -(grad_one + grad_two + grad_three)
    return (vertex_path, [grad_zero, grad_one, grad_two, grad_three])


def element_forces(offsets, displace, sign_y, sign_z):
    forces = {corner: jnp.zeros_like(displace[corner]) for corner in CORNER_LIST}
    for step_order in STEP_ORDERS:
        vertex_path, gradient_list = element_gradients(offsets, step_order, sign_y, sign_z)
        tensor = displace[vertex_path[0]][:, None] * gradient_list[0][None, :]
        for vertex in range(1, 4):
            tensor = (
                tensor + displace[vertex_path[vertex]][:, None] * gradient_list[vertex][None, :]
            )
        trace_sum = tensor[0, 0] + tensor[1, 1] + tensor[2, 2]
        symmetric = tensor + jnp.swapaxes(tensor, 0, 1)
        for vertex in range(4):
            gradient = gradient_list[vertex]
            nodal_force = LAMBDA_RATIO * trace_sum * gradient + jnp.sum(
                symmetric * gradient[None, :], axis=1
            )
            forces[vertex_path[vertex]] = forces[vertex_path[vertex]] + nodal_force
    return forces


def element_diagonal(offsets, sign_y, sign_z):
    result = {corner: jnp.zeros_like(offsets[corner]) for corner in CORNER_LIST}
    for step_order in STEP_ORDERS:
        vertex_path, gradient_list = element_gradients(offsets, step_order, sign_y, sign_z)
        for vertex in range(4):
            gradient = gradient_list[vertex]
            entry = (LAMBDA_RATIO + 1.0) * gradient * gradient + jnp.sum(
                gradient * gradient, axis=0
            )
            result[vertex_path[vertex]] = result[vertex_path[vertex]] + entry
    return result


def cell_corners(extended, count_y, count_z):
    return {
        corner: jnp.roll(
            extended[:, corner[1] : corner[1] + count_y, corner[2] : corner[2] + count_z, :],
            -corner[0],
            axis=3,
        )
        for corner in CORNER_LIST
    }


def corner_diagonal(offset_ext, masks, count_y, count_z):
    flip_y, flip_z, sign_y, sign_z = masks
    offsets = reflect_corners(cell_corners(offset_ext, count_y, count_z), flip_y, flip_z)
    return reflect_corners(element_diagonal(offsets, sign_y, sign_z), flip_y, flip_z)


def corner_forces(offset_ext, motion_ext, masks, count_y, count_z):
    flip_y, flip_z, sign_y, sign_z = masks
    offsets = reflect_corners(cell_corners(offset_ext, count_y, count_z), flip_y, flip_z)
    displace = reflect_corners(cell_corners(motion_ext, count_y, count_z), flip_y, flip_z)
    return reflect_corners(element_forces(offsets, displace, sign_y, sign_z), flip_y, flip_z)


def spread_sum(per_corner):
    pieces = [
        jnp.roll(
            jnp.pad(
                per_corner[corner],
                ((0, 0), (corner[1], 1 - corner[1]), (corner[2], 1 - corner[2]), (0, 0)),
            ),
            corner[0],
            axis=3,
        )
        for corner in CORNER_LIST
    ]
    return reduce(jnp.add, pieces)


def upper_ghosts(nodal_field):
    top_plane = from_behind(nodal_field[:, :, :1, :], "fluid", -1)
    widened = jnp.concatenate([nodal_field, top_plane], axis=2)
    row_part = from_behind(widened[:, :1], "struct", -1)
    return jnp.concatenate([widened, row_part], axis=1)


def fold_back(spread):
    count_y = spread.shape[1] - 1
    count_z = spread.shape[2] - 1
    row_part = from_behind(spread[:, count_y:], "struct", 1)
    folded = jnp.concatenate([spread[:, :1] + row_part, spread[:, 1:count_y]], axis=1)
    top_plane = from_behind(folded[:, :, count_z:], "fluid", 1)
    return jnp.concatenate([folded[:, :, :1] + top_plane, folded[:, :, 1:count_z]], axis=2)


def shards(shell_motion, owner, stencil_slot, stencil_weight, prev_motion, node_offset, cell_split):
    struct_count = lax.axis_size("struct")
    fluid_count = lax.axis_size("fluid")
    devices = struct_count * fluid_count
    capacity = 2 * shell_motion.shape[1] // devices
    targets = jnp.arange(devices, dtype=jnp.int32)
    owner_rows = owner[:, 0]
    onehot = (owner_rows[:, None] == targets[None, :]).astype(jnp.int32)
    before = jnp.cumsum(onehot, axis=0) - onehot
    slot_rank = jnp.sum(before * onehot, axis=1)
    slot_place = owner_rows * capacity + slot_rank
    packed = jnp.zeros((3, devices * capacity), jnp.float32).at[:, slot_place].set(shell_motion)
    received = lax.all_to_all(
        packed.reshape(3, devices, capacity),
        ("struct", "fluid"),
        split_axis=1,
        concat_axis=1,
        tiled=True,
    )
    received = received.reshape(3, devices * capacity)
    stencil_count, count_y, count_z, wall_width = stencil_slot.shape
    gathered = jnp.take(received, stencil_slot.reshape(-1), axis=1).reshape(
        3, stencil_count, count_y, count_z, wall_width
    )
    wall_values = jnp.sum(stencil_weight[None] * gathered, axis=1)
    motion = jnp.concatenate([wall_values, prev_motion[:, :, :, wall_width:]], axis=3)
    is_wall = (jnp.arange(motion.shape[3], dtype=jnp.int32) < wall_width)[None, None, None, :]
    masks = flip_masks(cell_split)
    offset_ext = upper_ghosts(node_offset)
    diagonal = fold_back(spread_sum(corner_diagonal(offset_ext, masks, count_y, count_z)))
    for sweep_index in range(SWEEPS):
        forces = fold_back(
            spread_sum(corner_forces(offset_ext, upper_ghosts(motion), masks, count_y, count_z))
        )
        motion = jnp.where(is_wall, motion, motion - RELAX_FACTOR * forces / diagonal)
    return motion


def solution(mesh):
    return jax.shard_map(
        shards,
        mesh=mesh,
        in_specs=(
            P(None, ("struct", "fluid")),
            P(("struct", "fluid"), None),
            P(None, "struct", "fluid", None),
            P(None, "struct", "fluid", None),
            P(None, "struct", "fluid", None),
            P(None, "struct", "fluid", None),
            P("struct", "fluid", None),
        ),
        out_specs=P(None, "struct", "fluid", None),
        check_vma=False,
    )
```

profile of v0, /device:TPU:0, one launch (start us, length us, event | category | flops | bytes accessed | tf_op | source)
XLA Modules:
  0.0 191.9 jit_solution(16414757542172310630)
XLA Ops:
  0.8 6.0 %collective-permute-start.2 = (f32[3,2,1,256]{3,2,1,0:T(1,128)S(1)}, f32[3,2,1,256]{3,2,1,0:T(1,128)S(1)}, u32[]{:S(2)}, u32[]{:S(2)}) collective-permute-start(f32[3,2,1,256]{3,2,1,0:T(1,128)S(1)} %slice.619), channel_id=1, source_target_pairs={{1,0},{2,1},{3,2},{4,3},{5,4},{6,5},{7,6},{8,7},{9,8},{10,9},{11,1... | collective-permute-start | bytes 18440 | tf_op jit(solution)/shard_map/ppermute | solution.py:19
  8.8 1.9 copy-done
  10.9 2.6 %broadcast_add_fusion = s32[128,64,128]{0,1,2:T(8,128)S(1)} fusion(s32[128,64,128]{0,1,2:T(8,128)} %copy-done, s32[128,64]{0,1:T(8,128)S(1)} %slice.845), kind=kLoop, calls=%fused_computation.12 | loop fusion | flops 1048576 | bytes 8421376 | tf_op jit(solution)/shard_map/reduce_window_sum
  13.5 2.4 %copy.1354 = s32[128,64,128]{0,2,1:T(8,128)S(1)} copy(s32[128,64,128]{0,1,2:T(8,128)S(1)} %broadcast_add_fusion) | data formatting | bytes 8388608 | tf_op jit(solution)/shard_map/reduce_window_sum
  16.0 2.8 %fusion.1 = s32[8192]{0:T(1024)S(1)} fusion(s32[128,64,128]{0,2,1:T(8,128)S(1)} %copy.1354, s32[8192]{0:T(1024)S(1)} %bitcast.86), kind=kLoop, calls=%fused_computation.4 | loop fusion | flops 5234688 | bytes 4259840 | tf_op jit(solution)/shard_map/reduce_sum | solution.py:186
  18.9 2.7 %copy.1355 = f32[8192,3]{1,0:T(8,128)} copy(f32[8192,3]{0,1:T(4,128)S(1)} %bitcast.88) | data formatting | bytes 196608 | tf_op args[0]
  21.5 24.5 %scatter_custom_fusion = f32[3,16384]{0,1:T(8,128)} fusion(s32[8192]{0:T(1024)S(1)} %bitcast.91, f32[8192,3]{1,0:T(8,128)} %copy.1355, f32[]{:T(128)} %constant.58.clone.1), kind=kCustom, calls=%fused_computation.10 | custom fusion | bytes 197120 | tf_op jit(solution)/shard_map/scatter | solution.py:188
  46.1 6.0 %copy.1356 = f32[3,128,128]{2,0,1:T(4,128)} copy(f32[3,128,128]{0,2,1:T(8,128)} %bitcast.81) | data formatting | bytes 393216 | tf_op jit(solution)/shard_map/reshape | solution.py:190
  52.0 5.2 %all-to-all-start = ((f32[3,128,128]{2,0,1:T(4,128)}), f32[3,128,128]{2,0,1:T(4,128)S(1)}, u32[]{:S(2)}, u32[]{:S(2)}) async-start(f32[3,128,128]{2,0,1:T(4,128)} %copy.1356), calls=%async_computation | async-start | bytes 524288 | tf_op jit(solution)/shard_map/all_to_all | solution.py:189
  57.6 2.2 %collective-permute-start.3 = (f32[3,1,9,256]{3,1,2,0:T(1,128)S(1)}, f32[3,1,9,256]{3,1,2,0:T(1,128)S(1)}, u32[]{:S(2)}, u32[]{:S(2)}) collective-permute-start(f32[3,1,9,256]{3,1,2,0:T(1,128)S(1)} %copy.1361), channel_id=1, source_target_pairs={{32,0},{64,32},{96,64},{0,96},{33,1},{65,33},{97,65},{1,97},{34,2}... | collective-permute-start | bytes 82952 | tf_op jit(solution)/shard_map/ppermute | solution.py:19
  60.0 2.0 %collective-permute-done.3 = f32[3,1,9,256]{3,1,2,0:T(1,128)S(1)} collective-permute-done((f32[3,1,9,256]{3,1,2,0:T(1,128)S(1)}, f32[3,1,9,256]{3,1,2,0:T(1,128)S(1)}, u32[]{:S(2)}, u32[]{:S(2)}) %collective-permute-start.3) | collective-permute-done | bytes 27680 | tf_op jit(solution)/shard_map/ppermute | solution.py:19
  62.5 5.5 %all-to-all-done = f32[3,128,128]{2,0,1:T(4,128)S(1)} async-done(((f32[3,128,128]{2,0,1:T(4,128)}), f32[3,128,128]{2,0,1:T(4,128)S(1)}, u32[]{:S(2)}, u32[]{:S(2)}) %all-to-all-start) | async-done | bytes 196640 | tf_op jit(solution)/shard_map/all_to_all | solution.py:189
  68.0 4.9 %copy.1357 = f32[3,128,128]{0,2,1:T(8,128)} copy(f32[3,128,128]{2,0,1:T(4,128)S(1)} %all-to-all-done) | data formatting | bytes 393216 | tf_op jit(solution)/shard_map/all_to_all | solution.py:189
  72.9 31.1 %gather_fusion = f32[8192,3]{1,0:T(8,128)} fusion(f32[3,16384]{0,1:T(8,128)} %bitcast.82, s32[8192]{0:T(1024)S(1)} %broadcast_clamp_fusion), kind=kCustom, calls=%fused_computation | custom fusion | bytes 229376 | tf_op jit(solution)/shard_map/jit(_take)/gather | solution.py:198
  104.0 6.1 %multiply_reduce_fusion = f32[3,2,8,128]{0,3,2,1:T(8,128)S(1)} fusion(f32[3,4,2,8,128]{0,4,3,2,1:T(8,128)} %bitcast.83, f32[4,2,8,128]{3,2,1,0:T(8,128)S(1)} %copy-done.5, pred[4,2,8,128]{3,2,1,0:T(8,128)(4,1)S(1)} %compare_and_fusion), kind=kLoop, calls=%fused_computation.5 | loop fusion | flops 67584 | bytes 163840 | tf_op jit(solution)/shard_map/reduce_sum | solution.py:201
  111.4 1.3 collective-permute-done
  112.8 1.5 collective-permute-start.1
  114.5 2.2 %collective-permute-done.1 = f32[3,1,9,256]{3,1,2,0:T(1,128)S(1)} collective-permute-done((f32[3,1,9,256]{3,1,2,0:T(1,128)S(1)}, f32[3,1,9,256]{3,1,2,0:T(1,128)S(1)}, u32[]{:S(2)}, u32[]{:S(2)}) %collective-permute-start.1) | collective-permute-done | bytes 27680 | tf_op jit(solution)/shard_map/ppermute | solution.py:19
  122.6 2.9 %collective-permute-done.6 = f32[3,1,9,256]{3,1,2,0:T(1,128)S(1)} collective-permute-done((f32[3,1,9,256]{3,1,2,0:T(1,128)S(1)}, f32[3,1,9,256]{3,1,2,0:T(1,128)S(1)}, u32[]{:S(2)}, u32[]{:S(2)}) %collective-permute-start.6) | collective-permute-done | bytes 27680 | tf_op jit(solution)/shard_map/ppermute | solution.py:19
  126.7 5.3 %collective-permute-done.7 = f32[3,2,1,256]{3,1,2,0:T(2,128)S(1)} collective-permute-done((f32[3,2,1,256]{3,1,2,0:T(2,128)S(1)}, f32[3,2,1,256]{3,1,2,0:T(2,128)S(1)}, u32[]{:S(2)}, u32[]{:S(2)}) %collective-permute-start.7) | collective-permute-done | bytes 6176 | tf_op jit(solution)/shard_map/ppermute | solution.py:19
  134.6 1.4 collective-permute-start.9
  136.2 2.4 %collective-permute-done.9 = f32[3,1,9,256]{3,1,2,0:T(1,128)S(1)} collective-permute-done((f32[3,1,9,256]{3,1,2,0:T(1,128)S(1)}, f32[3,1,9,256]{3,1,2,0:T(1,128)S(1)}, u32[]{:S(2)}, u32[]{:S(2)}) %collective-permute-start.9) | collective-permute-done | bytes 27680 | tf_op jit(solution)/shard_map/ppermute | solution.py:19
  141.0 4.8 %collective-permute-done.10 = f32[3,1,9,256]{3,1,2,0:T(1,128)S(1)} collective-permute-done((f32[3,1,9,256]{3,1,2,0:T(1,128)S(1)}, f32[3,1,9,256]{3,1,2,0:T(1,128)S(1)}, u32[]{:S(2)}, u32[]{:S(2)}) %collective-permute-start.10) | collective-permute-done | bytes 27680 | tf_op jit(solution)/shard_map/ppermute | solution.py:19
  146.1 6.3 %collective-permute-done.11 = f32[3,2,1,256]{3,1,2,0:T(2,128)S(1)} collective-permute-done((f32[3,2,1,256]{3,1,2,0:T(2,128)S(1)}, f32[3,2,1,256]{3,1,2,0:T(2,128)S(1)}, u32[]{:S(2)}, u32[]{:S(2)}) %collective-permute-start.11) | collective-permute-done | bytes 6176 | tf_op jit(solution)/shard_map/ppermute | solution.py:19
  153.9 1.4 collective-permute-start.13
  155.5 2.4 %collective-permute-done.13 = f32[3,1,9,256]{3,1,2,0:T(1,128)S(1)} collective-permute-done((f32[3,1,9,256]{3,1,2,0:T(1,128)S(1)}, f32[3,1,9,256]{3,1,2,0:T(1,128)S(1)}, u32[]{:S(2)}, u32[]{:S(2)}) %collective-permute-start.13) | collective-permute-done | bytes 27680 | tf_op jit(solution)/shard_map/ppermute | solution.py:19
  160.1 5.1 %collective-permute-done.14 = f32[3,1,9,256]{3,1,2,0:T(1,128)S(1)} collective-permute-done((f32[3,1,9,256]{3,1,2,0:T(1,128)S(1)}, f32[3,1,9,256]{3,1,2,0:T(1,128)S(1)}, u32[]{:S(2)}, u32[]{:S(2)}) %collective-permute-start.14) | collective-permute-done | bytes 27680 | tf_op jit(solution)/shard_map/ppermute | solution.py:19
  165.6 6.3 %collective-permute-done.15 = f32[3,2,1,256]{3,1,2,0:T(2,128)S(1)} collective-permute-done((f32[3,2,1,256]{3,1,2,0:T(2,128)S(1)}, f32[3,2,1,256]{3,1,2,0:T(2,128)S(1)}, u32[]{:S(2)}, u32[]{:S(2)}) %collective-permute-start.15) | collective-permute-done | bytes 6176 | tf_op jit(solution)/shard_map/ppermute | solution.py:19
  173.5 1.4 collective-permute-start.17
  175.0 2.4 %collective-permute-done.17 = f32[3,1,9,256]{3,1,2,0:T(1,128)S(1)} collective-permute-done((f32[3,1,9,256]{3,1,2,0:T(1,128)S(1)}, f32[3,1,9,256]{3,1,2,0:T(1,128)S(1)}, u32[]{:S(2)}, u32[]{:S(2)}) %collective-permute-start.17) | collective-permute-done | bytes 27680 | tf_op jit(solution)/shard_map/ppermute | solution.py:19
  179.6 5.1 %collective-permute-done.18 = f32[3,1,9,256]{3,1,2,0:T(1,128)S(1)} collective-permute-done((f32[3,1,9,256]{3,1,2,0:T(1,128)S(1)}, f32[3,1,9,256]{3,1,2,0:T(1,128)S(1)}, u32[]{:S(2)}, u32[]{:S(2)}) %collective-permute-start.18) | collective-permute-done | bytes 27680 | tf_op jit(solution)/shard_map/ppermute | solution.py:19
  184.9 6.3 %collective-permute-done.19 = f32[3,2,1,256]{3,1,2,0:T(2,128)S(1)} collective-permute-done((f32[3,2,1,256]{3,1,2,0:T(2,128)S(1)}, f32[3,2,1,256]{3,1,2,0:T(2,128)S(1)}, u32[]{:S(2)}, u32[]{:S(2)}) %collective-permute-start.19) | collective-permute-done | bytes 6176 | tf_op jit(solution)/shard_map/ppermute | solution.py:19
  (323 shorter events, 25.4 us)
Async XLA Ops:
  0.8 56.7 %collective-permute-start.2 = (f32[3,2,1,256]{3,2,1,0:T(1,128)S(1)}, f32[3,2,1,256]{3,2,1,0:T(1,128)S(1)}, u32[]{:S(2)}, u32[]{:S(2)}) collective-permute-start(f32[3,2,1,256]{3,2,1,0:T(1,128)S(1)} %slice.619), channel_id=1, source_target_pairs={{1,0},{2,1},{3,2},{4,3},{5,4},{6,5},{7,6},{8,7},{9,8},{10,9},{11,1... | collective-permute-start | bytes 18440 | tf_op jit(solution)/shard_map/ppermute | solution.py:19
  8.8 1.9 %copy-start = (s32[128,64,128]{0,1,2:T(8,128)}, s32[128,64,128]{0,1,2:T(8,128)S(1)}, u32[]{:S(2)}) copy-start(s32[128,64,128]{0,1,2:T(8,128)S(1)} %fusion.2) | copy-start | bytes 12582916
  13.5 2.5 %copy-start.2 = (s32[8192,1]{0,1:T(1,128)S(1)}, s32[8192,1]{0,1:T(1,128)}, u32[]{:S(2)}) copy-start(s32[8192,1]{0,1:T(1,128)} %param.8) | copy-start | bytes 98308
  15.9 2.9 %copy-start.3 = (f32[3,8192]{1,0:T(4,128)S(1)}, f32[3,8192]{1,0:T(4,128)}, u32[]{:S(2)}) copy-start(f32[3,8192]{1,0:T(4,128)} %param.7) | copy-start | bytes 294916
  46.1 11.2 %copy-start.6 = (s32[2,8,256]{2,1,0:T(8,128)S(1)}, s32[2,8,256]{2,1,0:T(8,128)}, u32[]{:S(2)}) copy-start(s32[2,8,256]{2,1,0:T(8,128)} %param.13) | copy-start | bytes 49156
  46.1 11.3 %copy-start.4 = (s32[4,2,8,128]{3,2,1,0:T(8,128)S(1)}, s32[4,2,8,128]{3,2,1,0:T(8,128)}, u32[]{:S(2)}) copy-start(s32[4,2,8,128]{3,2,1,0:T(8,128)} %param.9) | copy-start | bytes 98308
  46.1 11.4 %copy-start.1 = (f32[3,2,8,256]{3,2,1,0:T(8,128)S(1)}, f32[3,2,8,256]{3,2,1,0:T(8,128)}, u32[]{:S(2)}) copy-start(f32[3,2,8,256]{3,2,1,0:T(8,128)} %param.12) | copy-start | bytes 147460
  46.1 13.9 %copy-start.7 = (f32[3,2,8,256]{3,2,1,0:T(8,128)S(1)}, f32[3,2,8,256]{3,2,1,0:T(8,128)}, u32[]{:S(2)}) copy-start(f32[3,2,8,256]{3,2,1,0:T(8,128)} %param.11) | copy-start | bytes 147460
  52.0 16.0 %all-to-all-start = ((f32[3,128,128]{2,0,1:T(4,128)}), f32[3,128,128]{2,0,1:T(4,128)S(1)}, u32[]{:S(2)}, u32[]{:S(2)}) async-start(f32[3,128,128]{2,0,1:T(4,128)} %copy.1356), calls=%async_computation | async-start | bytes 524288 | tf_op jit(solution)/shard_map/all_to_all | solution.py:189
  57.6 4.4 %collective-permute-start.3 = (f32[3,1,9,256]{3,1,2,0:T(1,128)S(1)}, f32[3,1,9,256]{3,1,2,0:T(1,128)S(1)}, u32[]{:S(2)}, u32[]{:S(2)}) collective-permute-start(f32[3,1,9,256]{3,1,2,0:T(1,128)S(1)} %copy.1361), channel_id=1, source_target_pairs={{32,0},{64,32},{96,64},{0,96},{33,1},{65,33},{97,65},{1,97},{34,2}... | collective-permute-start | bytes 82952 | tf_op jit(solution)/shard_map/ppermute | solution.py:19
  62.5 41.5 %copy-start.5 = (f32[4,2,8,128]{3,2,1,0:T(8,128)S(1)}, f32[4,2,8,128]{3,2,1,0:T(8,128)}, u32[]{:S(2)}) copy-start(f32[4,2,8,128]{3,2,1,0:T(8,128)} %param.10) | copy-start | bytes 98308
  110.5 2.3 %collective-permute-start = (f32[3,2,1,256]{3,2,1,0:T(1,128)S(1)}, f32[3,2,1,256]{3,2,1,0:T(1,128)S(1)}, u32[]{:S(2)}, u32[]{:S(2)}) collective-permute-start(f32[3,2,1,256]{3,2,1,0:T(1,128)S(1)} %fusion.199), channel_id=1, source_target_pairs={{1,0},{2,1},{3,2},{4,3},{5,4},{6,5},{7,6},{8,7},{9,8},{10,9},{11,1... | collective-permute-start | bytes 18440 | tf_op jit(solution)/shard_map/ppermute | solution.py:19
  112.8 3.9 %collective-permute-start.1 = (f32[3,1,9,256]{3,1,2,0:T(1,128)S(1)}, f32[3,1,9,256]{3,1,2,0:T(1,128)S(1)}, u32[]{:S(2)}, u32[]{:S(2)}) collective-permute-start(f32[3,1,9,256]{3,1,2,0:T(1,128)S(1)} %copy.1359), channel_id=1, source_target_pairs={{32,0},{64,32},{96,64},{0,96},{33,1},{65,33},{97,65},{1,97},{34,2}... | collective-permute-start | bytes 82952 | tf_op jit(solution)/shard_map/ppermute | solution.py:19
  120.3 5.1 %collective-permute-start.6 = (f32[3,1,9,256]{3,1,2,0:T(1,128)S(1)}, f32[3,1,9,256]{3,1,2,0:T(1,128)S(1)}, u32[]{:S(2)}, u32[]{:S(2)}) collective-permute-start(f32[3,1,9,256]{3,1,2,0:T(1,128)S(1)} %copy.1370), channel_id=1, source_target_pairs={{96,0},{0,32},{32,64},{64,96},{97,1},{1,33},{33,65},{65,97},{98,2}... | collective-permute-start | bytes 82952 | tf_op jit(solution)/shard_map/ppermute | solution.py:19
  121.3 5.1 %collective-permute-start.4 = (f32[3,1,9,256]{3,1,2,0:T(1,128)S(1)}, f32[3,1,9,256]{3,1,2,0:T(1,128)S(1)}, u32[]{:S(2)}, u32[]{:S(2)}) collective-permute-start(f32[3,1,9,256]{3,1,2,0:T(1,128)S(1)} %copy.1364), channel_id=1, source_target_pairs={{96,0},{0,32},{32,64},{64,96},{97,1},{1,33},{33,65},{65,97},{98,2}... | collective-permute-start | bytes 82952 | tf_op jit(solution)/shard_map/ppermute | solution.py:19
  125.6 6.4 %collective-permute-start.7 = (f32[3,2,1,256]{3,1,2,0:T(2,128)S(1)}, f32[3,2,1,256]{3,1,2,0:T(2,128)S(1)}, u32[]{:S(2)}, u32[]{:S(2)}) collective-permute-start(f32[3,2,1,256]{3,1,2,0:T(2,128)S(1)} %pad_maximum_fusion.52), channel_id=1, source_target_pairs={{31,0},{0,1},{1,2},{2,3},{3,4},{4,5},{5,6},{6,7},{7,8},{8,9},{9,10... | collective-permute-start | bytes 18440 | tf_op jit(solution)/shard_map/ppermute | solution.py:19
  126.6 6.4 %collective-permute-start.5 = (f32[3,2,1,256]{3,1,2,0:T(2,128)S(1)}, f32[3,2,1,256]{3,1,2,0:T(2,128)S(1)}, u32[]{:S(2)}, u32[]{:S(2)}) collective-permute-start(f32[3,2,1,256]{3,1,2,0:T(2,128)S(1)} %pad_maximum_fusion.53), channel_id=1, source_target_pairs={{31,0},{0,1},{1,2},{2,3},{3,4},{4,5},{5,6},{6,7},{7,8},{8,9},{9,10... | collective-permute-start | bytes 18440 | tf_op jit(solution)/shard_map/ppermute | solution.py:19
  133.2 1.4 collective-permute-start.8
  134.6 3.9 %collective-permute-start.9 = (f32[3,1,9,256]{3,1,2,0:T(1,128)S(1)}, f32[3,1,9,256]{3,1,2,0:T(1,128)S(1)}, u32[]{:S(2)}, u32[]{:S(2)}) collective-permute-start(f32[3,1,9,256]{3,1,2,0:T(1,128)S(1)} %copy.1376), channel_id=1, source_target_pairs={{32,0},{64,32},{96,64},{0,96},{33,1},{65,33},{97,65},{1,97},{34,2}... | collective-permute-start | bytes 82952 | tf_op jit(solution)/shard_map/ppermute | solution.py:19
  140.7 5.1 %collective-permute-start.10 = (f32[3,1,9,256]{3,1,2,0:T(1,128)S(1)}, f32[3,1,9,256]{3,1,2,0:T(1,128)S(1)}, u32[]{:S(2)}, u32[]{:S(2)}) collective-permute-start(f32[3,1,9,256]{3,1,2,0:T(1,128)S(1)} %copy.1378), channel_id=1, source_target_pairs={{96,0},{0,32},{32,64},{64,96},{97,1},{1,33},{33,65},{65,97},{98,2}... | collective-permute-start | bytes 82952 | tf_op jit(solution)/shard_map/ppermute | solution.py:19
  146.0 6.4 %collective-permute-start.11 = (f32[3,2,1,256]{3,1,2,0:T(2,128)S(1)}, f32[3,2,1,256]{3,1,2,0:T(2,128)S(1)}, u32[]{:S(2)}, u32[]{:S(2)}) collective-permute-start(f32[3,2,1,256]{3,1,2,0:T(2,128)S(1)} %pad_maximum_fusion.51), channel_id=1, source_target_pairs={{31,0},{0,1},{1,2},{2,3},{3,4},{4,5},{5,6},{6,7},{7,8},{8,9},{9,10... | collective-permute-start | bytes 18440 | tf_op jit(solution)/shard_map/ppermute | solution.py:19
  152.5 1.4 collective-permute-start.12
  153.9 3.9 %collective-permute-start.13 = (f32[3,1,9,256]{3,1,2,0:T(1,128)S(1)}, f32[3,1,9,256]{3,1,2,0:T(1,128)S(1)}, u32[]{:S(2)}, u32[]{:S(2)}) collective-permute-start(f32[3,1,9,256]{3,1,2,0:T(1,128)S(1)} %copy.1384), channel_id=1, source_target_pairs={{32,0},{64,32},{96,64},{0,96},{33,1},{65,33},{97,65},{1,97},{34,2}... | collective-permute-start | bytes 82952 | tf_op jit(solution)/shard_map/ppermute | solution.py:19
  160.0 5.1 %collective-permute-start.14 = (f32[3,1,9,256]{3,1,2,0:T(1,128)S(1)}, f32[3,1,9,256]{3,1,2,0:T(1,128)S(1)}, u32[]{:S(2)}, u32[]{:S(2)}) collective-permute-start(f32[3,1,9,256]{3,1,2,0:T(1,128)S(1)} %copy.1386), channel_id=1, source_target_pairs={{96,0},{0,32},{32,64},{64,96},{97,1},{1,33},{33,65},{65,97},{98,2}... | collective-permute-start | bytes 82952 | tf_op jit(solution)/shard_map/ppermute | solution.py:19
  165.3 6.7 %collective-permute-start.15 = (f32[3,2,1,256]{3,1,2,0:T(2,128)S(1)}, f32[3,2,1,256]{3,1,2,0:T(2,128)S(1)}, u32[]{:S(2)}, u32[]{:S(2)}) collective-permute-start(f32[3,2,1,256]{3,1,2,0:T(2,128)S(1)} %pad_maximum_fusion.50), channel_id=1, source_target_pairs={{31,0},{0,1},{1,2},{2,3},{3,4},{4,5},{5,6},{6,7},{7,8},{8,9},{9,10... | collective-permute-start | bytes 18440 | tf_op jit(solution)/shard_map/ppermute | solution.py:19
  172.0 1.4 collective-permute-start.16
  173.5 3.9 %collective-permute-start.17 = (f32[3,1,9,256]{3,1,2,0:T(1,128)S(1)}, f32[3,1,9,256]{3,1,2,0:T(1,128)S(1)}, u32[]{:S(2)}, u32[]{:S(2)}) collective-permute-start(f32[3,1,9,256]{3,1,2,0:T(1,128)S(1)} %copy.1392), channel_id=1, source_target_pairs={{32,0},{64,32},{96,64},{0,96},{33,1},{65,33},{97,65},{1,97},{34,2}... | collective-permute-start | bytes 82952 | tf_op jit(solution)/shard_map/ppermute | solution.py:19
  179.5 5.1 %collective-permute-start.18 = (f32[3,1,9,256]{3,1,2,0:T(1,128)S(1)}, f32[3,1,9,256]{3,1,2,0:T(1,128)S(1)}, u32[]{:S(2)}, u32[]{:S(2)}) collective-permute-start(f32[3,1,9,256]{3,1,2,0:T(1,128)S(1)} %copy.1394), channel_id=1, source_target_pairs={{96,0},{0,32},{32,64},{64,96},{97,1},{1,33},{33,65},{65,97},{98,2}... | collective-permute-start | bytes 82952 | tf_op jit(solution)/shard_map/ppermute | solution.py:19
  184.8 6.4 %collective-permute-start.19 = (f32[3,2,1,256]{3,1,2,0:T(2,128)S(1)}, f32[3,2,1,256]{3,1,2,0:T(2,128)S(1)}, u32[]{:S(2)}, u32[]{:S(2)}) collective-permute-start(f32[3,2,1,256]{3,1,2,0:T(2,128)S(1)} %pad_maximum_fusion.49), channel_id=1, source_target_pairs={{31,0},{0,1},{1,2},{2,3},{3,4},{4,5},{5,6},{6,7},{7,8},{8,9},{9,10... | collective-permute-start | bytes 18440 | tf_op jit(solution)/shard_map/ppermute | solution.py:19
where the time goes:
time: 192 us
  local copies, waits for them, and re-layouts  78.6 us (41%)
  waiting for transfers between devices  66 us (34%)
  starting transfers between devices  23.5 us (12%)
  other arithmetic  21.9 us (11%)
    ppermute x20, waiting for transfers between devices, from_behind(): return lax.ppermute(block, axis, route)  60.4 us
    gather x1, local copies, waits for them, and re-layouts, shards(): jnp.take(received, stencil_slot.reshape(-1), axis=1)  31.1 us
    scatter x1, local copies, waits for them, and re-layouts, shards(): jnp.zeros((3, devices * capacity), jnp.float32).at[:, slot_place]  24.5 us
    ppermute x20, starting transfers between devices, from_behind(): return lax.ppermute(block, axis, route)  18.3 us
    reduce_sum x1, other arithmetic, shards(): wall_values = jnp.sum(stencil_weight[None] * gathered, axis=1)  6.12 us
    reshape x1, local copies, waits for them, and re-layouts, shards(): packed.reshape(3, devices, capacity)  5.95 us
    all_to_all x1, waiting for transfers between devices, shards(): lax.all_to_all(packed.reshape(3, devices, capacity), ('struct', 'fluid'),...  5.54 us
    all_to_all x1, starting transfers between devices, shards(): lax.all_to_all(packed.reshape(3, devices, capacity), ('struct', 'fluid'),...  5.25 us
  transfers between devices with their start and end apart: 21, of which 20 were waited for; matrix products, arithmetic and copies ran while one was open for 24% of the time, Pallas kernels for 0%

commit v1 on v0

--- a/solution.py
+++ b/solution.py
@@ -186,12 +186,21 @@
     slot_rank = jnp.sum(before * onehot, axis=1)
     slot_place = owner_rows * capacity + slot_rank
     packed = jnp.zeros((3, devices * capacity), jnp.float32).at[:, slot_place].set(shell_motion)
-    received = lax.all_to_all(
-        packed.reshape(3, devices, capacity),
-        ("struct", "fluid"),
-        split_axis=1,
-        concat_axis=1,
-        tiled=True,
+    received = jnp.concatenate(
+        jax.lax.all_to_all(
+            jnp.stack(
+                jnp.split(
+                    packed.reshape(3, devices, capacity),
+                    jax.lax.axis_size(("struct", "fluid")),
+                    axis=1,
+                ),
+                axis=0,
+            ),
+            ("struct", "fluid"),
+            0,
+            0,
+        ),
+        axis=1,
     )
     received = received.reshape(3, devices * capacity)
     stencil_count, count_y, count_z, wall_width = stencil_slot.shape

time: 192 us -> 331 us (1.72); the launches traced: 192 us -> 326 us
  local copies, waits for them, and re-layouts: 78.6 us -> 208 us
  starting transfers between devices: 23.5 us -> 36.8 us
  waiting for transfers between devices: 66 us -> 55.5 us
    unnamed x18 -> x144, local copies, waits for them, and re-layouts: 4.61 us -> 119 us
    split x0 -> x7, local copies, waits for them, and re-layouts: none -> 13.7 us  [shards(): jnp.split(packed.reshape(3, devices, capacity), jax.lax.axis_size(('struc...]
    another operation x3 -> x5, local copies, waits for them, and re-layouts: 2.44 us -> 11.5 us  [the longest x2 9.08 us: shards(): jnp.stack(jnp.split(packed.reshape(3, devices, capacity), jax.lax.axis_si...]
    ppermute x20, starting transfers between devices: 18.3 us -> 25.7 us  [from_behind(): return lax.ppermute(block, axis, route)]
    all_to_all x1, starting transfers between devices: 5.25 us -> 11.1 us  [shards(): jax.lax.all_to_all(jnp.stack(jnp.split(packed.reshape(3, devices, capacit...]
    all_to_all x1, waiting for transfers between devices: 5.54 us -> 0.01 us  [shards(): jax.lax.all_to_all(jnp.stack(jnp.split(packed.reshape(3, devices, capacit...]
    ppermute x20, waiting for transfers between devices: 60.4 us -> 55.5 us  [from_behind(): return lax.ppermute(block, axis, route)]
    all_to_all x1 -> x0, local copies, waits for them, and re-layouts: 4.86 us -> none  [shards(): lax.all_to_all(packed.reshape(3, devices, capacity), ('struct', 'fluid'),...]
  transfers between devices with their start and end apart: 21 -> 21, of which waited for: 20 -> 19; matrix products, arithmetic and copies ran while one was open for 24% -> 1% of each run, Pallas kernels for 0% -> 0%
where the time goes in v1:
time: 331 us; the launch traced here: 326 us
  local copies, waits for them, and re-layouts  208 us (63%)
  waiting for transfers between devices  55.5 us (17%)
  starting transfers between devices  36.8 us (11%)
  other arithmetic  23.5 us (7%)
    unnamed x144, local copies, waits for them, and re-layouts  119 us
    ppermute x20, waiting for transfers between devices, from_behind(): return lax.ppermute(block, axis, route)  55.5 us
    gather x1, local copies, waits for them, and re-layouts, shards(): jnp.take(received, stencil_slot.reshape(-1), axis=1)  31.1 us
    ppermute x20, starting transfers between devices, from_behind(): return lax.ppermute(block, axis, route)  25.7 us
    scatter x1, local copies, waits for them, and re-layouts, shards(): jnp.zeros((3, devices * capacity), jnp.float32).at[:, slot_place]  24.5 us
    split x7, local copies, waits for them, and re-layouts, shards(): jnp.split(packed.reshape(3, devices, capacity), jax.lax.axis_size(('struc...  13.7 us
    all_to_all x1, starting transfers between devices, shards(): jax.lax.all_to_all(jnp.stack(jnp.split(packed.reshape(3, devices, capacit...  11.1 us
    another operation x2, local copies, waits for them, and re-layouts, shards(): jnp.stack(jnp.split(packed.reshape(3, devices, capacity), jax.lax.axis_si...  9.08 us
  transfers between devices with their start and end apart: 21, of which 19 were waited for; matrix products, arithmetic and copies ran while one was open for 1% of the time, Pallas kernels for 0%

profile of v1, /device:TPU:0, one launch (start us, length us, event | category | flops | bytes accessed | tf_op | source)
XLA Modules:
  0.0 326.2 jit_solution(17515380364196647504)
XLA Ops:
  2.0 1.9 copy-done
  4.0 2.6 broadcast_add_fusion
  6.7 2.4 copy.1994
  9.1 2.8 fusion.1
  12.1 2.7 copy.1995
  14.7 24.5 %scatter_custom_fusion = f32[3,16384]{0,1:T(8,128)} fusion(s32[8192]{0:T(1024)S(1)} %bitcast.227, f32[8192,3]{1,0:T(8,128)} %copy.1995, f32[]{:T(128)} %constant.58.clone.1), kind=kCustom, calls=%fused_computation.10 | custom fusion | bytes 197120 | tf_op jit(solution)/shard_map/scatter | solution.py:188
  39.3 2.4 fusion.248
  41.6 2.4 fusion.247
  44.0 2.4 fusion.252
  46.4 2.5 fusion.251
  167.0 8.2 %stack.432 = f32[128,3,1,128]{3,0,2,1:T(8,128)S(1)} concatenate(f32[1,3,1,128]{3,0,2,1:T(1,128)S(1)} %bitcast.355, f32[1,3,1,128]{3,0,2,1:T(1,128)S(1)} %bitcast.342, f32[1,3,1,128]{3,0,2,1:T(1,128)S(1)} %bitcast.343, f32[1,3,1,128]{3,0,2,1:T(1,128)S(1)} %bitcast.344, f32[1,3,1,128]{3,0,2,1:T(1,128)S(1)} %bitcast.345, f32[1,3,1,128]{3,0,2,1:T(1,128)S(1)} %bitcast.346, ...), dimensions={0} | concatenate | bytes 393216 | tf_op jit(solution)/shard_map/stack | solution.py:191
  176.1 11.1 %all-to-all-start = ((f32[128,3,1,128]{3,2,1,0:T(1,128)}), f32[128,3,1,128]{3,2,1,0:T(1,128)S(1)}, u32[]{:S(2)}, u32[]{:S(2)}) async-start(f32[128,3,1,128]{3,2,1,0:T(1,128)} %copy.2124), calls=%async_computation | async-start | bytes 393216 | tf_op jit(solution)/shard_map/all_to_all | solution.py:190
  187.3 5.0 %collective-permute-start.2 = (f32[3,2,1,256]{3,2,1,0:T(1,128)S(1)}, f32[3,2,1,256]{3,2,1,0:T(1,128)S(1)}, u32[]{:S(2)}, u32[]{:S(2)}) collective-permute-start(f32[3,2,1,256]{3,2,1,0:T(1,128)S(1)} %slice.619), channel_id=1, source_target_pairs={{1,0},{2,1},{3,2},{4,3},{5,4},{6,5},{7,6},{8,7},{9,8},{10,9},{11,1... | collective-permute-start | bytes 18440 | tf_op jit(solution)/shard_map/ppermute | solution.py:19
  194.0 2.8 collective-permute-start.3
  198.9 4.7 %copy.2125 = f32[3,128,1,128]{0,3,1,2:T(8,128)} copy(f32[3,128,1,128]{3,2,0,1:T(1,128)S(1)} %bitcast.220) | data formatting | bytes 393216 | tf_op jit(solution)/shard_map/reshape | solution.py:189
  203.6 31.1 %gather_fusion = f32[8192,3]{1,0:T(8,128)} fusion(f32[3,16384]{0,1:T(8,128)} %bitcast.217, s32[8192]{0:T(1024)S(1)} %broadcast_clamp_fusion), kind=kCustom, calls=%fused_computation | custom fusion | bytes 229376 | tf_op jit(solution)/shard_map/jit(_take)/gather | solution.py:207
  234.7 6.1 %multiply_reduce_fusion = f32[3,2,8,128]{0,3,2,1:T(8,128)S(1)} fusion(f32[3,4,2,8,128]{0,4,3,2,1:T(8,128)} %bitcast.218, f32[4,2,8,128]{3,2,1,0:T(8,128)S(1)} %copy-done.4, pred[4,2,8,128]{3,2,1,0:T(8,128)(4,1)S(1)} %compare_and_fusion), kind=kLoop, calls=%fused_computation.5 | loop fusion | flops 67584 | bytes 163840 | tf_op jit(solution)/shard_map/reduce_sum | solution.py:210
  241.2 3.9 %collective-permute-start = (f32[3,2,1,256]{3,2,1,0:T(1,128)S(1)}, f32[3,2,1,256]{3,2,1,0:T(1,128)S(1)}, u32[]{:S(2)}, u32[]{:S(2)}) collective-permute-start(f32[3,2,1,256]{3,2,1,0:T(1,128)S(1)} %fusion.199), channel_id=1, source_target_pairs={{1,0},{2,1},{3,2},{4,3},{5,4},{6,5},{7,6},{8,7},{9,8},{10,9},{11,1... | collective-permute-start | bytes 18440 | tf_op jit(solution)/shard_map/ppermute | solution.py:19
  246.5 3.3 %collective-permute-start.1 = (f32[3,1,9,256]{3,1,2,0:T(1,128)S(1)}, f32[3,1,9,256]{3,1,2,0:T(1,128)S(1)}, u32[]{:S(2)}, u32[]{:S(2)}) collective-permute-start(f32[3,1,9,256]{3,1,2,0:T(1,128)S(1)} %copy.2127), channel_id=1, source_target_pairs={{32,0},{64,32},{96,64},{0,96},{33,1},{65,33},{97,65},{1,97},{34,2}... | collective-permute-start | bytes 82952 | tf_op jit(solution)/shard_map/ppermute | solution.py:19
  255.3 2.0 collective-permute-start.4
  257.3 3.1 collective-permute-done.6
  261.2 5.7 %collective-permute-done.7 = f32[3,2,1,256]{3,1,2,0:T(2,128)S(1)} collective-permute-done((f32[3,2,1,256]{3,1,2,0:T(2,128)S(1)}, f32[3,2,1,256]{3,1,2,0:T(2,128)S(1)}, u32[]{:S(2)}, u32[]{:S(2)}) %collective-permute-start.7) | collective-permute-done | bytes 6176 | tf_op jit(solution)/shard_map/ppermute | solution.py:19
  269.1 2.1 collective-permute-start.9
  271.3 1.7 collective-permute-done.9
  276.6 3.7 %collective-permute-done.10 = f32[3,1,9,256]{3,1,2,0:T(1,128)S(1)} collective-permute-done((f32[3,1,9,256]{3,1,2,0:T(1,128)S(1)}, f32[3,1,9,256]{3,1,2,0:T(1,128)S(1)}, u32[]{:S(2)}, u32[]{:S(2)}) %collective-permute-start.10) | collective-permute-done | bytes 27680 | tf_op jit(solution)/shard_map/ppermute | solution.py:19
  280.6 6.3 %collective-permute-done.11 = f32[3,2,1,256]{3,1,2,0:T(2,128)S(1)} collective-permute-done((f32[3,2,1,256]{3,1,2,0:T(2,128)S(1)}, f32[3,2,1,256]{3,1,2,0:T(2,128)S(1)}, u32[]{:S(2)}, u32[]{:S(2)}) %collective-permute-start.11) | collective-permute-done | bytes 6176 | tf_op jit(solution)/shard_map/ppermute | solution.py:19
  288.4 2.1 collective-permute-start.13
  294.7 4.9 %collective-permute-done.14 = f32[3,1,9,256]{3,1,2,0:T(1,128)S(1)} collective-permute-done((f32[3,1,9,256]{3,1,2,0:T(1,128)S(1)}, f32[3,1,9,256]{3,1,2,0:T(1,128)S(1)}, u32[]{:S(2)}, u32[]{:S(2)}) %collective-permute-start.14) | collective-permute-done | bytes 27680 | tf_op jit(solution)/shard_map/ppermute | solution.py:19
  299.9 6.3 %collective-permute-done.15 = f32[3,2,1,256]{3,1,2,0:T(2,128)S(1)} collective-permute-done((f32[3,2,1,256]{3,1,2,0:T(2,128)S(1)}, f32[3,2,1,256]{3,1,2,0:T(2,128)S(1)}, u32[]{:S(2)}, u32[]{:S(2)}) %collective-permute-start.15) | collective-permute-done | bytes 6176 | tf_op jit(solution)/shard_map/ppermute | solution.py:19
  307.7 2.1 collective-permute-start.17
  313.9 5.1 %collective-permute-done.18 = f32[3,1,9,256]{3,1,2,0:T(1,128)S(1)} collective-permute-done((f32[3,1,9,256]{3,1,2,0:T(1,128)S(1)}, f32[3,1,9,256]{3,1,2,0:T(1,128)S(1)}, u32[]{:S(2)}, u32[]{:S(2)}) %collective-permute-start.18) | collective-permute-done | bytes 27680 | tf_op jit(solution)/shard_map/ppermute | solution.py:19
  319.2 6.3 %collective-permute-done.19 = f32[3,2,1,256]{3,1,2,0:T(2,128)S(1)} collective-permute-done((f32[3,2,1,256]{3,1,2,0:T(2,128)S(1)}, f32[3,2,1,256]{3,1,2,0:T(2,128)S(1)}, u32[]{:S(2)}, u32[]{:S(2)}) %collective-permute-start.19) | collective-permute-done | bytes 6176 | tf_op jit(solution)/shard_map/ppermute | solution.py:19
  (457 shorter events, 150.2 us)
Async XLA Ops:
  2.0 1.9 copy-start
  6.7 2.5 copy-start.2
  9.1 2.9 copy-start.3
  90.8 96.4 %copy-start.1 = (f32[3,2,8,256]{3,2,1,0:T(8,128)S(1)}, f32[3,2,8,256]{3,2,1,0:T(8,128)}, u32[]{:S(2)}) copy-start(f32[3,2,8,256]{3,2,1,0:T(8,128)} %param.12) | copy-start | bytes 147460
  95.3 98.6 %copy-start.5 = (s32[2,8,256]{2,1,0:T(8,128)S(1)}, s32[2,8,256]{2,1,0:T(8,128)}, u32[]{:S(2)}) copy-start(s32[2,8,256]{2,1,0:T(8,128)} %param.13) | copy-start | bytes 49156
  162.8 34.1 %copy-start.6 = (f32[3,2,8,256]{3,2,1,0:T(8,128)S(1)}, f32[3,2,8,256]{3,2,1,0:T(8,128)}, u32[]{:S(2)}) copy-start(f32[3,2,8,256]{3,2,1,0:T(8,128)} %param.11) | copy-start | bytes 147460
  176.1 22.8 %all-to-all-start = ((f32[128,3,1,128]{3,2,1,0:T(1,128)}), f32[128,3,1,128]{3,2,1,0:T(1,128)S(1)}, u32[]{:S(2)}, u32[]{:S(2)}) async-start(f32[128,3,1,128]{3,2,1,0:T(1,128)} %copy.2124), calls=%async_computation | async-start | bytes 393216 | tf_op jit(solution)/shard_map/all_to_all | solution.py:190
  187.3 6.6 %collective-permute-start.2 = (f32[3,2,1,256]{3,2,1,0:T(1,128)S(1)}, f32[3,2,1,256]{3,2,1,0:T(1,128)S(1)}, u32[]{:S(2)}, u32[]{:S(2)}) collective-permute-start(f32[3,2,1,256]{3,2,1,0:T(1,128)S(1)} %slice.619), channel_id=1, source_target_pairs={{1,0},{2,1},{3,2},{4,3},{5,4},{6,5},{7,6},{8,7},{9,8},{10,9},{11,1... | collective-permute-start | bytes 18440 | tf_op jit(solution)/shard_map/ppermute | solution.py:19
  194.0 4.3 %collective-permute-start.3 = (f32[3,1,9,256]{3,1,2,0:T(1,128)S(1)}, f32[3,1,9,256]{3,1,2,0:T(1,128)S(1)}, u32[]{:S(2)}, u32[]{:S(2)}) collective-permute-start(f32[3,1,9,256]{3,1,2,0:T(1,128)S(1)} %copy.2129), channel_id=1, source_target_pairs={{32,0},{64,32},{96,64},{0,96},{33,1},{65,33},{97,65},{1,97},{34,2}... | collective-permute-start | bytes 82952 | tf_op jit(solution)/shard_map/ppermute | solution.py:19
  198.9 35.8 %copy-start.4 = (f32[4,2,8,128]{3,2,1,0:T(8,128)S(1)}, f32[4,2,8,128]{3,2,1,0:T(8,128)}, u32[]{:S(2)}) copy-start(f32[4,2,8,128]{3,2,1,0:T(8,128)} %param.10) | copy-start | bytes 98308
  241.2 5.2 %collective-permute-start = (f32[3,2,1,256]{3,2,1,0:T(1,128)S(1)}, f32[3,2,1,256]{3,2,1,0:T(1,128)S(1)}, u32[]{:S(2)}, u32[]{:S(2)}) collective-permute-start(f32[3,2,1,256]{3,2,1,0:T(1,128)S(1)} %fusion.199), channel_id=1, source_target_pairs={{1,0},{2,1},{3,2},{4,3},{5,4},{6,5},{7,6},{8,7},{9,8},{10,9},{11,1... | collective-permute-start | bytes 18440 | tf_op jit(solution)/shard_map/ppermute | solution.py:19
  246.5 4.8 %collective-permute-start.1 = (f32[3,1,9,256]{3,1,2,0:T(1,128)S(1)}, f32[3,1,9,256]{3,1,2,0:T(1,128)S(1)}, u32[]{:S(2)}, u32[]{:S(2)}) collective-permute-start(f32[3,1,9,256]{3,1,2,0:T(1,128)S(1)} %copy.2127), channel_id=1, source_target_pairs={{32,0},{64,32},{96,64},{0,96},{33,1},{65,33},{97,65},{1,97},{34,2}... | collective-permute-start | bytes 82952 | tf_op jit(solution)/shard_map/ppermute | solution.py:19
  254.9 5.4 %collective-permute-start.6 = (f32[3,1,9,256]{3,1,2,0:T(1,128)S(1)}, f32[3,1,9,256]{3,1,2,0:T(1,128)S(1)}, u32[]{:S(2)}, u32[]{:S(2)}) collective-permute-start(f32[3,1,9,256]{3,1,2,0:T(1,128)S(1)} %copy.2138), channel_id=1, source_target_pairs={{96,0},{0,32},{32,64},{64,96},{97,1},{1,33},{33,65},{65,97},{98,2}... | collective-permute-start | bytes 82952 | tf_op jit(solution)/shard_map/ppermute | solution.py:19
  255.3 5.6 %collective-permute-start.4 = (f32[3,1,9,256]{3,1,2,0:T(1,128)S(1)}, f32[3,1,9,256]{3,1,2,0:T(1,128)S(1)}, u32[]{:S(2)}, u32[]{:S(2)}) collective-permute-start(f32[3,1,9,256]{3,1,2,0:T(1,128)S(1)} %copy.2132), channel_id=1, source_target_pairs={{96,0},{0,32},{32,64},{64,96},{97,1},{1,33},{33,65},{65,97},{98,2}... | collective-permute-start | bytes 82952 | tf_op jit(solution)/shard_map/ppermute | solution.py:19
  260.5 6.4 %collective-permute-start.7 = (f32[3,2,1,256]{3,1,2,0:T(2,128)S(1)}, f32[3,2,1,256]{3,1,2,0:T(2,128)S(1)}, u32[]{:S(2)}, u32[]{:S(2)}) collective-permute-start(f32[3,2,1,256]{3,1,2,0:T(2,128)S(1)} %pad_maximum_fusion.52), channel_id=1, source_target_pairs={{31,0},{0,1},{1,2},{2,3},{3,4},{4,5},{5,6},{6,7},{7,8},{8,9},{9,10... | collective-permute-start | bytes 18440 | tf_op jit(solution)/shard_map/ppermute | solution.py:19
  261.1 6.4 %collective-permute-start.5 = (f32[3,2,1,256]{3,1,2,0:T(2,128)S(1)}, f32[3,2,1,256]{3,1,2,0:T(2,128)S(1)}, u32[]{:S(2)}, u32[]{:S(2)}) collective-permute-start(f32[3,2,1,256]{3,1,2,0:T(2,128)S(1)} %pad_maximum_fusion.53), channel_id=1, source_target_pairs={{31,0},{0,1},{1,2},{2,3},{3,4},{4,5},{5,6},{6,7},{7,8},{8,9},{9,10... | collective-permute-start | bytes 18440 | tf_op jit(solution)/shard_map/ppermute | solution.py:19
  267.6 1.4 collective-permute-start.8
  269.1 3.9 %collective-permute-start.9 = (f32[3,1,9,256]{3,1,2,0:T(1,128)S(1)}, f32[3,1,9,256]{3,1,2,0:T(1,128)S(1)}, u32[]{:S(2)}, u32[]{:S(2)}) collective-permute-start(f32[3,1,9,256]{3,1,2,0:T(1,128)S(1)} %copy.2144), channel_id=1, source_target_pairs={{32,0},{64,32},{96,64},{0,96},{33,1},{65,33},{97,65},{1,97},{34,2}... | collective-permute-start | bytes 82952 | tf_op jit(solution)/shard_map/ppermute | solution.py:19
  275.2 5.1 %collective-permute-start.10 = (f32[3,1,9,256]{3,1,2,0:T(1,128)S(1)}, f32[3,1,9,256]{3,1,2,0:T(1,128)S(1)}, u32[]{:S(2)}, u32[]{:S(2)}) collective-permute-start(f32[3,1,9,256]{3,1,2,0:T(1,128)S(1)} %copy.2146), channel_id=1, source_target_pairs={{96,0},{0,32},{32,64},{64,96},{97,1},{1,33},{33,65},{65,97},{98,2}... | collective-permute-start | bytes 82952 | tf_op jit(solution)/shard_map/ppermute | solution.py:19
  280.4 6.4 %collective-permute-start.11 = (f32[3,2,1,256]{3,1,2,0:T(2,128)S(1)}, f32[3,2,1,256]{3,1,2,0:T(2,128)S(1)}, u32[]{:S(2)}, u32[]{:S(2)}) collective-permute-start(f32[3,2,1,256]{3,1,2,0:T(2,128)S(1)} %pad_maximum_fusion.51), channel_id=1, source_target_pairs={{31,0},{0,1},{1,2},{2,3},{3,4},{4,5},{5,6},{6,7},{7,8},{8,9},{9,10... | collective-permute-start | bytes 18440 | tf_op jit(solution)/shard_map/ppermute | solution.py:19
  287.0 1.4 collective-permute-start.12
  288.4 3.9 %collective-permute-start.13 = (f32[3,1,9,256]{3,1,2,0:T(1,128)S(1)}, f32[3,1,9,256]{3,1,2,0:T(1,128)S(1)}, u32[]{:S(2)}, u32[]{:S(2)}) collective-permute-start(f32[3,1,9,256]{3,1,2,0:T(1,128)S(1)} %copy.2152), channel_id=1, source_target_pairs={{32,0},{64,32},{96,64},{0,96},{33,1},{65,33},{97,65},{1,97},{34,2}... | collective-permute-start | bytes 82952 | tf_op jit(solution)/shard_map/ppermute | solution.py:19
  294.5 5.1 %collective-permute-start.14 = (f32[3,1,9,256]{3,1,2,0:T(1,128)S(1)}, f32[3,1,9,256]{3,1,2,0:T(1,128)S(1)}, u32[]{:S(2)}, u32[]{:S(2)}) collective-permute-start(f32[3,1,9,256]{3,1,2,0:T(1,128)S(1)} %copy.2154), channel_id=1, source_target_pairs={{96,0},{0,32},{32,64},{64,96},{97,1},{1,33},{33,65},{65,97},{98,2}... | collective-permute-start | bytes 82952 | tf_op jit(solution)/shard_map/ppermute | solution.py:19
  299.7 6.4 %collective-permute-start.15 = (f32[3,2,1,256]{3,1,2,0:T(2,128)S(1)}, f32[3,2,1,256]{3,1,2,0:T(2,128)S(1)}, u32[]{:S(2)}, u32[]{:S(2)}) collective-permute-start(f32[3,2,1,256]{3,1,2,0:T(2,128)S(1)} %pad_maximum_fusion.50), channel_id=1, source_target_pairs={{31,0},{0,1},{1,2},{2,3},{3,4},{4,5},{5,6},{6,7},{7,8},{8,9},{9,10... | collective-permute-start | bytes 18440 | tf_op jit(solution)/shard_map/ppermute | solution.py:19
  306.3 1.4 collective-permute-start.16
  307.7 3.9 %collective-permute-start.17 = (f32[3,1,9,256]{3,1,2,0:T(1,128)S(1)}, f32[3,1,9,256]{3,1,2,0:T(1,128)S(1)}, u32[]{:S(2)}, u32[]{:S(2)}) collective-permute-start(f32[3,1,9,256]{3,1,2,0:T(1,128)S(1)} %copy.2160), channel_id=1, source_target_pairs={{32,0},{64,32},{96,64},{0,96},{33,1},{65,33},{97,65},{1,97},{34,2}... | collective-permute-start | bytes 82952 | tf_op jit(solution)/shard_map/ppermute | solution.py:19
  313.8 5.1 %collective-permute-start.18 = (f32[3,1,9,256]{3,1,2,0:T(1,128)S(1)}, f32[3,1,9,256]{3,1,2,0:T(1,128)S(1)}, u32[]{:S(2)}, u32[]{:S(2)}) collective-permute-start(f32[3,1,9,256]{3,1,2,0:T(1,128)S(1)} %copy.2162), channel_id=1, source_target_pairs={{96,0},{0,32},{32,64},{64,96},{97,1},{1,33},{33,65},{65,97},{98,2}... | collective-permute-start | bytes 82952 | tf_op jit(solution)/shard_map/ppermute | solution.py:19
  319.0 6.4 %collective-permute-start.19 = (f32[3,2,1,256]{3,1,2,0:T(2,128)S(1)}, f32[3,2,1,256]{3,1,2,0:T(2,128)S(1)}, u32[]{:S(2)}, u32[]{:S(2)}) collective-permute-start(f32[3,2,1,256]{3,1,2,0:T(2,128)S(1)} %pad_maximum_fusion.49), channel_id=1, source_target_pairs={{31,0},{0,1},{1,2},{2,3},{3,4},{4,5},{5,6},{6,7},{7,8},{8,9},{9,10... | collective-permute-start | bytes 18440 | tf_op jit(solution)/shard_map/ppermute | solution.py:19
